TPU v7x, 256 devices: a whole 4x4x8 slice. The times are simulated.
256 devices in a mesh: dom: 128 (over y, x, z), col: 2 (over core).
Axes of the slice: x: 4, y: 4, z: 8, core: 2. Of those that a mesh axis runs over, the one named last changes fastest.
Arguments:
- features: bfloat16 [131072, 256], P(('dom', 'col')), may hold values from -6 to 6
- weight: bfloat16 [256, 256], replicated, may hold values from -0.375 to 0.375
- cotangent: bfloat16 [131072, 256], P(('dom', 'col')), may hold values from -6 to 6
- tile_values: bfloat16 [10240, 128, 128], P(('dom', 'col')), may hold values from -0.15625 to 0.15625
- tile_rows: int32 [10240], P(('dom', 'col')), may hold values from 0 to 7
- tile_cols: int32 [10240], P(('dom', 'col')), may hold values from 0 to 131, as said below
- tile_count: int32 [256], P(('dom', 'col')), may hold values from 20 to 40, as said below
- send_blocks: int32 [256, 128], P(('dom', 'col')), may hold values from 0 to 3
Outputs:
- output_rows: bfloat16 [131072, 256], P(('dom', 'col'))
- feature_grad: bfloat16 [131072, 256], P(('dom', 'col'))
- weight_grad: float32 [256, 256], replicated
Inputs may be any that keep to these rules, and one draw needn't show every extreme that they name: `tile_cols`: A value v below 4 names the device's own row block v; a value 4 + s names the row block that the device of partition s with the same col index sends to this partition; no receive slot is named by two tiles of one device. Only the first tile_count slots of a device's tiles are live; some device has all 40 live.
All inputs are finite; a program needn't handle non-finite values.
Results may differ from a plain program's by a relative error of at most 0.0049.
Values may be sent and summed in bfloat16 or wider, within the bound.
No kernel may reach another device: no remote copies, remote signals or barrier semaphores. Data moves between devices by JAX's collectives and lax.ppermute only.
A program may use at most 128 MiB of HBM per device.

v0:
```python
import jax
import jax.numpy as jnp
from jax import lax
from jax.sharding import PartitionSpec as P


def in_one_piece(arrays, axis, split_dim, concat_dim, along):
    ends, at = ([], 0)
    for a in arrays[:-1]:
        at += a.shape[along]
        ends.append(at)
    both = jnp.concatenate(arrays, axis=along)
    return tuple(
        jnp.split(
            lax.all_to_all(both, axis, split_axis=split_dim, concat_axis=concat_dim, tiled=True),
            ends,
            axis=along,
        )
    )


def local(features, weight, cotangent, tile_values, tile_rows, tile_cols, tile_count, send_blocks):
    block_size = tile_values.shape[1]
    half_blocks = features.shape[0] // block_size
    width_in = features.shape[1]
    peer_count = send_blocks.shape[1]
    all_blocks = half_blocks * lax.axis_size("col")
    node_total = features.shape[0] * lax.axis_size("col") * lax.axis_size("dom")
    own_blocks = features.reshape(half_blocks, block_size, width_in)
    outgoing = own_blocks[send_blocks[0]]
    incoming = lax.all_to_all(outgoing, "dom", split_axis=0, concat_axis=0, tiled=True)
    sources = jnp.concatenate([own_blocks, incoming], axis=0)
    live_bool = jnp.arange(tile_values.shape[0], dtype=jnp.int32) < tile_count[0]
    live_mask = live_bool.astype(jnp.bfloat16)
    masked_tiles = tile_values * live_mask[:, None, None]
    picked = sources[tile_cols]
    products = jnp.einsum("tij,tjf->tif", masked_tiles, picked, preferred_element_type=jnp.float32)
    partial_value = jax.ops.segment_sum(products, tile_rows, num_segments=all_blocks)
    summed = lax.psum_scatter(partial_value, "col", scatter_dimension=0, tiled=True)
    hidden = summed.astype(jnp.bfloat16).reshape(half_blocks * block_size, width_in)
    output_rows = jnp.dot(hidden, weight, preferred_element_type=jnp.float32).astype(jnp.bfloat16)
    own_grad = lax.dot_general(
        cotangent, weight, (((1,), (1,)), ((), ())), preferred_element_type=jnp.float32
    ).astype(jnp.bfloat16)
    own_grad = own_grad.reshape(half_blocks, block_size, width_in)
    grad_blocks = lax.all_gather(own_grad, "col", axis=0, tiled=True)
    chosen = grad_blocks[tile_rows]
    is_local = tile_cols < half_blocks
    local_tiles = masked_tiles * is_local.astype(jnp.bfloat16)[:, None, None]
    back_terms = jnp.einsum("tji,tjf->tif", local_tiles, chosen, preferred_element_type=jnp.float32)
    local_ids = jnp.where(is_local, tile_cols, 0)
    own_part = jax.ops.segment_sum(back_terms, local_ids, num_segments=half_blocks)
    slot_ids = half_blocks + jnp.arange(peer_count, dtype=jnp.int32)
    matches = ((tile_cols[:, None] == slot_ids[None, :]) & live_bool[:, None]).astype(jnp.bfloat16)
    slot_tiles = jnp.einsum(
        "ts,tij->sij", matches, tile_values, preferred_element_type=jnp.float32
    ).astype(jnp.bfloat16)
    slot_grads = jnp.einsum(
        "ts,tjf->sjf", matches, chosen, preferred_element_type=jnp.float32
    ).astype(jnp.bfloat16)
    back_tiles, back_grads = in_one_piece((slot_tiles, slot_grads), "dom", 0, 0, 2)
    remote_terms = jnp.einsum(
        "sji,sjf->sif", back_tiles, back_grads, preferred_element_type=jnp.float32
    )
    grad_total = own_part + jax.ops.segment_sum(
        remote_terms, send_blocks[0], num_segments=half_blocks
    )
    feature_grad = grad_total.astype(jnp.bfloat16).reshape(half_blocks * block_size, width_in)
    local_weight = lax.dot_general(
        hidden, cotangent, (((0,), (0,)), ((), ())), preferred_element_type=jnp.float32
    )
    local_weight = local_weight * jnp.float32(1.0 / node_total**0.5)
    weight_grad = lax.psum(local_weight, ("dom", "col"))
    return (output_rows, feature_grad, weight_grad)


def solution(mesh):
    return jax.shard_map(
        local,
        mesh=mesh,
        in_specs=(
            P(("dom", "col"), None),
            P(),
            P(("dom", "col"), None),
            P(("dom", "col"), None, None),
            P(("dom", "col")),
            P(("dom", "col")),
            P(("dom", "col")),
            P(("dom", "col"), None),
        ),
        out_specs=(P(("dom", "col"), None), P(("dom", "col"), None), P()),
        check_vma=False,
    )
```

profile of v0, /device:TPU:2, one launch (start us, length us, event | category | flops | bytes accessed | tf_op | source)
XLA Modules:
  0.0 573.9 jit_solution(5552977802668099284)
XLA Ops:
  7.2 0.0 copy-start
  7.2 0.7 fusion.21
  7.9 7.5 %gather_fusion = bf16[128,128,256]{2,1,0:T(8,128)(2,1)} fusion(bf16[4,128,256]{2,1,0:T(8,128)(2,1)} %bitcast.25, s32[1024]{0:T(1024)S(1)} %pad_clamp_fusion.2), kind=kCustom, calls=%fused_computation | custom fusion | bytes 16777728 | tf_op jit(solution)/shard_map/gather | solution.py:30
  15.3 0.0 copy-start.5
  15.3 0.0 copy-start.8
  15.4 16.0 %all-to-all-start = ((bf16[128,128,256]{2,1,0:T(8,128)(2,1)}), bf16[128,128,256]{2,1,0:T(8,128)(2,1)}, u32[]{:S(2)}, u32[]{:S(2)}) async-start(bf16[128,128,256]{2,1,0:T(8,128)(2,1)} %gather_fusion), calls=%async_computation | async-start | bytes 16777216 | tf_op jit(solution)/shard_map/all_to_all | solution.py:31
  32.0 0.0 copy-done.5
  32.0 0.0 copy-done.8
  32.0 3.8 convolution_convert_fusion.1
  35.8 0.0 copy-start.9
  35.8 0.0 copy-start.7
  35.8 6.4 %copy.26 = bf16[128,128,128]{2,0,1:T(8,128)(2,1)} copy(bf16[128,128,128]{0,2,1:T(8,128)(2,1)} %convolution_convert_fusion.1) | data formatting | bytes 8388608 | tf_op jit(solution)/shard_map/convert_element_type | solution.py:57
  42.2 0.0 copy-done.9
  42.2 0.0 copy-done
  42.2 0.0 copy-done.7
  42.3 0.3 convolution_convert_fusion.2
  42.5 2.4 all_gather.3
  44.9 0.7 gather_fusion.2
  45.6 0.0 copy-start.3
  45.6 0.0 copy-start.4
  45.6 2.5 convolution_convert_fusion
  48.1 0.0 copy-done.3
  48.1 0.7 copy-done.4
  48.7 2.3 pad_maximum_fusion
  51.0 29.1 %copy.27 = bf16[128,128,384]{2,1,0:T(8,128)(2,1)} copy(bf16[128,128,384]{2,0,1:T(8,128)(2,1)S(1)} %pad_maximum_fusion) | data formatting | bytes 25165824 | tf_op jit(solution)/shard_map/concatenate | solution.py:12
  80.1 0.0 copy-start.1
  80.1 136.3 %all-to-all-done = bf16[128,128,256]{2,1,0:T(8,128)(2,1)} async-done(((bf16[128,128,256]{2,1,0:T(8,128)(2,1)}), bf16[128,128,256]{2,1,0:T(8,128)(2,1)}, u32[]{:S(2)}, u32[]{:S(2)}) %all-to-all-start) | async-done | bytes 8388640 | tf_op jit(solution)/shard_map/all_to_all | solution.py:31
  216.4 11.2 %all-to-all-start.1 = ((bf16[128,128,384]{2,1,0:T(8,128)(2,1)}), bf16[128,128,384]{2,1,0:T(8,128)(2,1)}, u32[]{:S(2)}, u32[]{:S(2)}) async-start(bf16[128,128,384]{2,1,0:T(8,128)(2,1)} %copy.27), calls=%async_computation.2 | async-start | bytes 25165824 | tf_op jit(solution)/shard_map/all_to_all | solution.py:15
  227.6 0.3 reduce-scatter.2.cloned.1.call-start
  227.9 0.0 copy-done.1
  227.9 7.5 %pad_maximum_fusion.1 = bf16[132,128,256]{2,1,0:T(8,128)(2,1)} fusion(bf16[128,128,256]{2,1,0:T(8,128)(2,1)} %all-to-all-done, bf16[4,128,256]{2,1,0:T(8,128)(2,1)S(1)} %bitcast.26), kind=kLoop, calls=%fused_computation.7 | loop fusion | flops 4325376 | bytes 17301504 | tf_op jit(solution)/shard_map/concatenate | solution.py:32
  235.4 0.0 copy-start.6
  235.4 6.0 %gather_fusion.1 = bf16[40,128,256]{2,1,0:T(8,128)(2,1)} fusion(bf16[132,128,256]{2,1,0:T(8,128)(2,1)} %pad_maximum_fusion.1, s32[1024]{0:T(1024)S(1)} %pad_clamp_fusion.1), kind=kCustom, calls=%fused_computation.1 | custom fusion | bytes 5243040 | tf_op jit(solution)/shard_map/gather | solution.py:36
  241.5 0.0 copy-done.6
  241.5 0.0 copy-start.10
  241.5 4.9 fusion.8
  246.4 0.1 broadcast_in_dim.12
  246.5 0.0 copy-done.10
  246.5 9.0 %scatter_fusion = f32[8,128,256]{2,1,0:T(8,128)S(1)} fusion(f32[8,128,256]{2,1,0:T(8,128)S(1)} %broadcast_in_dim.12, s32[40]{0:T(128)S(1)} %copy-done.10, f32[40,128,256]{2,1,0:T(8,128)} %fusion.8), kind=kCustom, calls=%fused_computation.3 | custom fusion | flops 1310720 | bytes 15728800 | tf_op jit(solution)/shard_map/scatter-add | solution.py:38
  255.6 0.0 copy-start.2
  255.6 1.0 copy-done.2
  256.5 0.0 reduce-scatter.2.cloned.1.call-update
  256.6 0.0 all-reduce.2.cloned.1.call-start
  256.6 5.3 fusion.5
  261.9 9.1 %scatter_fusion.1 = f32[4,128,256]{2,1,0:T(8,128)S(1)} fusion(f32[4,128,256]{2,1,0:T(8,128)S(1)} %broadcast.41.clone, s32[40]{0:T(128)S(1)} %get-tuple-element.3, f32[40,128,256]{2,1,0:T(8,128)} %fusion.5), kind=kCustom, calls=%fused_computation.4 | custom fusion | flops 1310720 | bytes 15728800 | tf_op jit(solution)/shard_map/scatter-add | solution.py:52
  271.1 0.9 reduce-scatter.2.cloned.1.call-done
  272.0 1.1 convert_element_type.30
  273.0 1.0 convolution_multiply_fusion
  274.0 0.0 all-reduce.2.cloned.1.call-update
  274.0 0.9 convolution_convert_fusion.3
  275.0 0.0 copy-start.11
  275.0 227.1 %all-to-all-done.1 = bf16[128,128,384]{2,1,0:T(8,128)(2,1)} async-done(((bf16[128,128,384]{2,1,0:T(8,128)(2,1)}), bf16[128,128,384]{2,1,0:T(8,128)(2,1)}, u32[]{:S(2)}, u32[]{:S(2)}) %all-to-all-start.1) | async-done | bytes 12582944 | tf_op jit(solution)/shard_map/all_to_all | solution.py:15
  502.1 12.8 %fusion = f32[128,128,256]{2,1,0:T(8,128)} fusion(bf16[128,128,384]{2,1,0:T(8,128)(2,1)} %all-to-all-done.1), kind=kOutput, calls=%fused_computation.8 | convolution fusion | flops 1073741824 | bytes 29360128 | tf_op jit(solution)/shard_map/sji,sjf->sif/dot_general | solution.py:62
  514.9 0.0 copy-done.11
  514.9 24.1 %scatter_fusion.2 = f32[4,128,256]{2,1,0:T(8,128)S(1)} fusion(f32[4,128,256]{2,1,0:T(8,128)S(1)} %broadcast.41.clone.1, s32[128]{0:T(128)S(1)} %bitcast.31, f32[128,128,256]{2,1,0:T(8,128)} %fusion), kind=kCustom, calls=%fused_computation.5 | custom fusion | flops 4194304 | bytes 50332160 | tf_op jit(solution)/shard_map/scatter-add | solution.py:65
  539.0 0.8 add_convert_fusion
  539.8 25.6 %all-reduce.2.cloned.1.call-done = f32[256,256]{1,0:T(8,128)} async-done(((f32[256,256]{1,0:T(8,128)}), f32[256,256]{1,0:T(8,128)}) %all-reduce.2.cloned.1.call-update) | async-done | bytes 262160 | tf_op jit(solution)/shard_map/psum | solution.py:73
  565.4 1.7 copy.40
  (11 shorter events, 0.1 us)
Async XLA Ops:
  7.2 35.1 %copy-start = (bf16[512,256]{1,0:T(8,128)(2,1)S(1)}, bf16[512,256]{1,0:T(8,128)(2,1)}, u32[]{:S(2)}) copy-start(bf16[512,256]{1,0:T(8,128)(2,1)} %param.10) | copy-start | bytes 786436
  15.3 16.7 %copy-start.5 = (bf16[40,128,128]{2,1,0:T(8,128)(2,1)S(1)}, bf16[40,128,128]{2,1,0:T(8,128)(2,1)}, u32[]{:S(2)}) copy-start(bf16[40,128,128]{2,1,0:T(8,128)(2,1)} %param.11) | copy-start | bytes 3932164
  15.3 16.7 %copy-start.8 = (s32[40]{0:T(128)S(1)}, s32[40]{0:T(128)}, u32[]{:S(2)}) copy-start(s32[40]{0:T(128)} %param.13) | copy-start | bytes 484
  15.4 201.0 %all-to-all-start = ((bf16[128,128,256]{2,1,0:T(8,128)(2,1)}), bf16[128,128,256]{2,1,0:T(8,128)(2,1)}, u32[]{:S(2)}, u32[]{:S(2)}) async-start(bf16[128,128,256]{2,1,0:T(8,128)(2,1)} %gather_fusion), calls=%async_computation | async-start | bytes 16777216 | tf_op jit(solution)/shard_map/all_to_all | solution.py:31
  35.8 6.4 %copy-start.9 = (s32[40]{0:T(128)S(1)}, s32[40]{0:T(128)}, u32[]{:S(2)}) copy-start(s32[40]{0:T(128)} %param.12) | copy-start | bytes 484
  35.8 6.4 %copy-start.7 = (bf16[256,256]{1,0:T(8,128)(2,1)S(1)}, bf16[256,256]{1,0:T(8,128)(2,1)}, u32[]{:S(2)}) copy-start(bf16[256,256]{1,0:T(8,128)(2,1)} %param.9) | copy-start | bytes 393220
  45.6 2.5 copy-start.3
  45.6 3.1 copy-start.4
  80.1 147.8 %copy-start.1 = (bf16[512,256]{1,0:T(8,128)(2,1)S(1)}, bf16[512,256]{1,0:T(8,128)(2,1)}, u32[]{:S(2)}) copy-start(bf16[512,256]{1,0:T(8,128)(2,1)} %param.8) | copy-start | bytes 786436
  216.4 285.7 %all-to-all-start.1 = ((bf16[128,128,384]{2,1,0:T(8,128)(2,1)}), bf16[128,128,384]{2,1,0:T(8,128)(2,1)}, u32[]{:S(2)}, u32[]{:S(2)}) async-start(bf16[128,128,384]{2,1,0:T(8,128)(2,1)} %copy.27), calls=%async_computation.2 | async-start | bytes 25165824 | tf_op jit(solution)/shard_map/all_to_all | solution.py:15
  227.6 44.4 %reduce-scatter.2.cloned.1.call-start = ((), (), s32[]{:S(2)}) async-start(), calls=%async_computation.3 | async-start | bytes 1572864 | tf_op jit(solution)/shard_map/reduce_scatter | solution.py:39
  235.4 6.0 %copy-start.6 = (bf16[40,128,128]{2,1,0:T(8,128)(2,1)S(1)}, bf16[40,128,128]{2,1,0:T(8,128)(2,1)}, u32[]{:S(2)}) copy-start(bf16[40,128,128]{2,1,0:T(8,128)(2,1)} %param.11) | copy-start | bytes 3932164
  241.5 5.0 copy-start.10
  255.6 1.0 copy-start.2
  256.6 308.9 %all-reduce.2.cloned.1.call-start = ((), (), s32[]{:S(2)}) async-start(), calls=%async_computation.4 | async-start | bytes 524288 | tf_op jit(solution)/shard_map/psum | solution.py:73
  275.0 239.9 %copy-start.11 = (s32[1,128]{1,0:T(1,128)S(1)}, s32[1,128]{1,0:T(1,128)}, u32[]{:S(2)}) copy-start(s32[1,128]{1,0:T(1,128)} %param.15) | copy-start | bytes 1540
Sparse Core Ops, SparseCore 0:
  256.7 15.2 reduce-scatter.1
  278.9 286.4 all-reduce.1
where the time goes:
time: 575 us; the launch traced here: 574 us
  waiting for transfers between devices  390 us (68%)
  other arithmetic  54.6 us (9%)
  local copies, waits for them, and re-layouts  53.2 us (9%)
  matrix products  31.4 us (5%)
  starting transfers between devices  27.5 us (5%)
  between operations  14.9 us (3%)
    all_to_all x1, waiting for transfers between devices, in_one_piece(): lax.all_to_all(both, axis, split_axis=split_dim, concat_axis=concat_dim,...  227 us
    all_to_all x1, waiting for transfers between devices, local(): lax.all_to_all(outgoing, 'dom', split_axis=0, concat_axis=0, tiled=True)  136 us
    concatenate x1, local copies, waits for them, and re-layouts, in_one_piece(): both = jnp.concatenate(arrays, axis=along)  29.1 us
    psum x1, waiting for transfers between devices, local(): weight_grad = lax.psum(local_weight, ('dom', 'col'))  25.6 us
    scatter-add x1, other arithmetic, local(): jax.ops.segment_sum(remote_terms, send_blocks[0], num_segments=half_blocks)  24.1 us
    all_to_all x1, starting transfers between devices, local(): lax.all_to_all(outgoing, 'dom', split_axis=0, concat_axis=0, tiled=True)  16 us
    dot_general x1, matrix products, local(): jnp.einsum('sji,sjf->sif', back_tiles, back_grads, preferred_element_type...  12.8 us
  transfers between devices with their start and end apart: 4, of which 4 were waited for; matrix products, arithmetic and copies ran while one was open for 22% of the time, Pallas kernels for 0%

commit v1 on v0

--- a/solution.py
+++ b/solution.py
@@ -70,7 +70,8 @@
         hidden, cotangent, (((0,), (0,)), ((), ())), preferred_element_type=jnp.float32
     )
     local_weight = local_weight * jnp.float32(1.0 / node_total**0.5)
-    weight_grad = lax.psum(local_weight, ("dom", "col"))
+    shards = lax.all_gather(local_weight, ("dom", "col"))
+    weight_grad = jnp.sum(shards, axis=0)
     return (output_rows, feature_grad, weight_grad)
 
 

time: 575 us -> 782 us (1.36)
  waiting for transfers between devices: 390 us -> 570 us
  other arithmetic: 54.6 us -> 76.7 us
    all_to_all x1, waiting for transfers between devices: 227 us -> 377 us  [in_one_piece(): lax.all_to_all(both, axis, split_axis=split_dim, concat_axis=concat_dim,...]
    all_to_all x1, waiting for transfers between devices: 136 us -> 184 us  [local(): lax.all_to_all(outgoing, 'dom', split_axis=0, concat_axis=0, tiled=True)]
    psum x1 -> x0, waiting for transfers between devices: 25.6 us -> none  [local(): weight_grad = lax.psum(local_weight, ('dom', 'col'))]
    reduce_sum x0 -> x1, other arithmetic: none -> 21.8 us  [local(): weight_grad = jnp.sum(shards, axis=0)]
    reduce_scatter x1, waiting for transfers between devices: 0.91 us -> 9.87 us  [local(): lax.psum_scatter(partial_value, 'col', scatter_dimension=0, tiled=True)]
  transfers between devices with their start and end apart: 4 -> 4, of which waited for: 4 -> 3; matrix products, arithmetic and copies ran while one was open for 22% -> 13% of each run, Pallas kernels for 0% -> 0%
where the time goes in v1:
time: 782 us; the launch traced here: 778 us
  waiting for transfers between devices  570 us (73%)
  other arithmetic  76.7 us (10%)
  local copies, waits for them, and re-layouts  51.5 us (7%)
  matrix products  32.2 us (4%)
  starting transfers between devices  30.2 us (4%)
  between operations  14.9 us (2%)
    all_to_all x1, waiting for transfers between devices, in_one_piece(): lax.all_to_all(both, axis, split_axis=split_dim, concat_axis=concat_dim,...  377 us
    all_to_all x1, waiting for transfers between devices, local(): lax.all_to_all(outgoing, 'dom', split_axis=0, concat_axis=0, tiled=True)  184 us
    concatenate x1, local copies, waits for them, and re-layouts, in_one_piece(): both = jnp.concatenate(arrays, axis=along)  29 us
    scatter-add x1, other arithmetic, local(): jax.ops.segment_sum(remote_terms, send_blocks[0], num_segments=half_blocks)  24.1 us
    reduce_sum x1, other arithmetic, local(): weight_grad = jnp.sum(shards, axis=0)  21.8 us
    all_to_all x1, starting transfers between devices, local(): lax.all_to_all(outgoing, 'dom', split_axis=0, concat_axis=0, tiled=True)  16 us
  transfers between devices with their start and end apart: 4, of which 3 were waited for; matrix products, arithmetic and copies ran while one was open for 13% of the time, Pallas kernels for 0%

profile of v1, /device:TPU:2, one launch (start us, length us, event | category | flops | bytes accessed | tf_op | source)
XLA Modules:
  0.0 778.1 jit_solution(4187768351390402524)
XLA Ops:
  7.2 0.0 copy-start
  7.2 0.7 fusion.21
  7.9 7.4 gather_fusion
  15.3 0.0 copy-start.9
  15.3 0.0 copy-start.2
  15.3 16.0 %all-to-all-start = ((bf16[128,128,256]{2,1,0:T(8,128)(2,1)}), bf16[128,128,256]{2,1,0:T(8,128)(2,1)}, u32[]{:S(2)}, u32[]{:S(2)}) async-start(bf16[128,128,256]{2,1,0:T(8,128)(2,1)} %gather_fusion), calls=%async_computation | async-start | bytes 16777216 | tf_op jit(solution)/shard_map/all_to_all | solution.py:31
  31.3 0.0 reduce-scatter.2.cloned.1.call-start
  32.0 0.0 copy-done.9
  32.0 0.5 compare_select_fusion.3
  32.6 183.8 %all-to-all-done = bf16[128,128,256]{2,1,0:T(8,128)(2,1)} async-done(((bf16[128,128,256]{2,1,0:T(8,128)(2,1)}), bf16[128,128,256]{2,1,0:T(8,128)(2,1)}, u32[]{:S(2)}, u32[]{:S(2)}) %all-to-all-start) | async-done | bytes 8388640 | tf_op jit(solution)/shard_map/all_to_all | solution.py:31
  216.4 0.0 copy-done.2
  216.4 7.5 pad_maximum_fusion.1
  223.9 0.0 copy-start.5
  223.9 6.0 gather_fusion.1
  229.9 0.0 copy-done.5
  229.9 0.0 copy-start.12
  229.9 4.9 fusion.8
  234.8 0.1 broadcast_in_dim.12
  234.9 0.0 copy-done.12
  234.9 9.0 %scatter_fusion = f32[8,128,256]{2,1,0:T(8,128)S(1)} fusion(f32[8,128,256]{2,1,0:T(8,128)S(1)} %broadcast_in_dim.12, s32[40]{0:T(128)S(1)} %copy-done.12, f32[40,128,256]{2,1,0:T(8,128)} %fusion.8), kind=kCustom, calls=%fused_computation.3 | custom fusion | flops 1310720 | bytes 15728800 | tf_op jit(solution)/shard_map/scatter-add | solution.py:38
  243.9 0.0 copy-start.3
  244.0 1.0 copy-done.3
  244.9 0.0 reduce-scatter.2.cloned.1.call-update
  244.9 0.0 all-gather.3.cloned.1.call-start
  245.0 9.9 %reduce-scatter.2.cloned.1.call-done = f32[4,128,256]{2,1,0:T(8,128)} async-done(((f32[8,128,256]{2,1,0:T(8,128)}), f32[4,128,256]{2,1,0:T(8,128)}) %reduce-scatter.2.cloned.1.call-update) | async-done | bytes 524304 | tf_op jit(solution)/shard_map/reduce_scatter | solution.py:39
  254.9 1.1 convert_element_type.30
  255.9 0.0 copy-start.6
  255.9 0.7 copy-done.6
  256.6 0.0 copy-done
  256.6 1.0 convolution_multiply_fusion
  257.6 0.0 all-gather.3.cloned.1.call-update
  257.7 0.0 copy-start.10
  257.7 3.8 convolution_convert_fusion.1
  261.5 0.0 copy-start.8
  261.5 6.5 copy.26
  268.0 0.0 copy-done.10
  268.0 0.0 copy-done.8
  268.0 0.3 convolution_convert_fusion.2
  268.2 0.0 copy-start.11
  268.3 2.4 all_gather.9
  270.6 0.7 gather_fusion.2
  271.3 0.0 copy-done.11
  271.4 0.0 copy-start.4
  271.4 2.5 convolution_convert_fusion
  273.8 0.0 copy-done.4
  273.8 2.3 pad_maximum_fusion
  276.1 29.0 %copy.27 = bf16[128,128,384]{2,1,0:T(8,128)(2,1)} copy(bf16[128,128,384]{2,0,1:T(8,128)(2,1)S(1)} %pad_maximum_fusion) | data formatting | bytes 25165824 | tf_op jit(solution)/shard_map/concatenate | solution.py:12
  305.1 14.2 %all-to-all-start.1 = ((bf16[128,128,384]{2,1,0:T(8,128)(2,1)}), bf16[128,128,384]{2,1,0:T(8,128)(2,1)}, u32[]{:S(2)}, u32[]{:S(2)}) async-start(bf16[128,128,384]{2,1,0:T(8,128)(2,1)} %copy.27), calls=%async_computation.2 | async-start | bytes 25165824 | tf_op jit(solution)/shard_map/all_to_all | solution.py:15
  319.3 0.0 copy-start.13
  319.3 5.1 fusion.5
  324.4 0.0 copy-done.13
  324.4 0.0 copy-start.7
  324.4 9.0 %scatter_fusion.1 = f32[4,128,256]{2,1,0:T(8,128)S(1)} fusion(f32[4,128,256]{2,1,0:T(8,128)S(1)} %broadcast.41.clone, s32[40]{0:T(128)S(1)} %copy-done.13, f32[40,128,256]{2,1,0:T(8,128)} %fusion.5), kind=kCustom, calls=%fused_computation.4 | custom fusion | flops 1310720 | bytes 15728800 | tf_op jit(solution)/shard_map/scatter-add | solution.py:52
  333.5 0.0 copy-done.7
  333.5 0.9 convolution_convert_fusion.3
  334.4 0.0 copy-start.14
  334.4 376.5 %all-to-all-done.1 = bf16[128,128,384]{2,1,0:T(8,128)(2,1)} async-done(((bf16[128,128,384]{2,1,0:T(8,128)(2,1)}), bf16[128,128,384]{2,1,0:T(8,128)(2,1)}, u32[]{:S(2)}, u32[]{:S(2)}) %all-to-all-start.1) | async-done | bytes 12582944 | tf_op jit(solution)/shard_map/all_to_all | solution.py:15
  710.9 13.7 %fusion = f32[128,128,256]{2,1,0:T(8,128)} fusion(bf16[128,128,384]{2,1,0:T(8,128)(2,1)} %all-to-all-done.1), kind=kOutput, calls=%fused_computation.8 | convolution fusion | flops 1073741824 | bytes 29360128 | tf_op jit(solution)/shard_map/sji,sjf->sif/dot_general | solution.py:62
  724.7 0.0 copy-done.14
  724.7 24.1 %scatter_fusion.2 = f32[4,128,256]{2,1,0:T(8,128)S(1)} fusion(f32[4,128,256]{2,1,0:T(8,128)S(1)} %broadcast.41.clone.1, s32[128]{0:T(128)S(1)} %bitcast.32, f32[128,128,256]{2,1,0:T(8,128)} %fusion), kind=kCustom, calls=%fused_computation.5 | custom fusion | flops 4194304 | bytes 50332160 | tf_op jit(solution)/shard_map/scatter-add | solution.py:65
  748.8 0.8 add_convert_fusion
  749.5 0.0 copy-start.1
  749.5 21.8 %reduce_sum.9 = f32[256,256]{1,0:T(8,128)} reduce(f32[256,256,256]{2,1,0:T(8,128)} %bitcast.9, f32[]{:T(128)} %constant.6.clone.1), dimensions={0}, to_apply=%region_4.5 | reduce | flops 16711680 | bytes 67371008 | tf_op jit(solution)/shard_map/reduce_sum | solution.py:74
  771.3 0.0 copy-done.1
  (11 shorter events, 0.1 us)
Async XLA Ops:
  7.2 249.5 %copy-start = (bf16[512,256]{1,0:T(8,128)(2,1)S(1)}, bf16[512,256]{1,0:T(8,128)(2,1)}, u32[]{:S(2)}) copy-start(bf16[512,256]{1,0:T(8,128)(2,1)} %param.10) | copy-start | bytes 786436
  15.3 16.7 %copy-start.9 = (s32[40]{0:T(128)S(1)}, s32[40]{0:T(128)}, u32[]{:S(2)}) copy-start(s32[40]{0:T(128)} %param.13) | copy-start | bytes 484
  15.3 201.0 %copy-start.2 = (bf16[512,256]{1,0:T(8,128)(2,1)S(1)}, bf16[512,256]{1,0:T(8,128)(2,1)}, u32[]{:S(2)}) copy-start(bf16[512,256]{1,0:T(8,128)(2,1)} %param.8) | copy-start | bytes 786436
  15.3 201.0 %all-to-all-start = ((bf16[128,128,256]{2,1,0:T(8,128)(2,1)}), bf16[128,128,256]{2,1,0:T(8,128)(2,1)}, u32[]{:S(2)}, u32[]{:S(2)}) async-start(bf16[128,128,256]{2,1,0:T(8,128)(2,1)} %gather_fusion), calls=%async_computation | async-start | bytes 16777216 | tf_op jit(solution)/shard_map/all_to_all | solution.py:31
  31.3 223.5 %reduce-scatter.2.cloned.1.call-start = ((), (), s32[]{:S(2)}) async-start(), calls=%async_computation.3 | async-start | bytes 1572864 | tf_op jit(solution)/shard_map/reduce_scatter | solution.py:39
  223.9 6.0 copy-start.5
  229.9 5.0 copy-start.12
  243.9 1.0 copy-start.3
  244.9 504.6 %all-gather.3.cloned.1.call-start = ((), (), s32[]{:S(2)}) async-start(), calls=%async_computation.4 | async-start | bytes 67371008 | tf_op jit(solution)/shard_map/all_gather | solution.py:73
  255.9 0.7 copy-start.6
  257.7 10.3 %copy-start.10 = (pred[40]{0:T(512)(128)(4,1)}, pred[40]{0:T(512)(128)(4,1)S(1)}, u32[]{:S(2)}) copy-start(pred[40]{0:T(512)(128)(4,1)S(1)} %iota_compare_fusion) | copy-start | bytes 124
  261.5 6.5 copy-start.8
  268.2 3.1 copy-start.11
  271.4 2.5 copy-start.4
  305.1 405.8 %all-to-all-start.1 = ((bf16[128,128,384]{2,1,0:T(8,128)(2,1)}), bf16[128,128,384]{2,1,0:T(8,128)(2,1)}, u32[]{:S(2)}, u32[]{:S(2)}) async-start(bf16[128,128,384]{2,1,0:T(8,128)(2,1)} %copy.27), calls=%async_computation.2 | async-start | bytes 25165824 | tf_op jit(solution)/shard_map/all_to_all | solution.py:15
  319.3 5.1 copy-start.13
  324.4 9.0 %copy-start.7 = (bf16[4,128,256]{2,1,0:T(8,128)(2,1)S(1)}, bf16[4,128,256]{2,1,0:T(8,128)(2,1)}, u32[]{:S(2)}) copy-start(bf16[4,128,256]{2,1,0:T(8,128)(2,1)} %copy-done.6) | copy-start | bytes 786436
  334.4 390.3 %copy-start.14 = (s32[1,128]{1,0:T(1,128)S(1)}, s32[1,128]{1,0:T(1,128)}, u32[]{:S(2)}) copy-start(s32[1,128]{1,0:T(1,128)} %param.15) | copy-start | bytes 1540
  749.5 21.8 %copy-start.1 = (bf16[512,256]{1,0:T(8,128)(2,1)S(1)}, bf16[512,256]{1,0:T(8,128)(2,1)}, u32[]{:S(2)}) copy-start(bf16[512,256]{1,0:T(8,128)(2,1)} %param.10) | copy-start | bytes 786436
Sparse Core Ops, SparseCore 0:
  245.1 9.7 reduce-scatter.1
  259.2 463.4 all-gather.2
